TPU v7x, 32 devices: a whole 2x2x4 slice. The times are simulated.
32 devices in a mesh: gx: 4 (over x, core), gy: 2 (over y), gz: 4 (over z).
Axes of the slice: x: 2, y: 2, z: 4, core: 2. Of those that a mesh axis runs over, the one named last changes fastest.
Arguments:
- tokens: bfloat16 [24, 6144], P(('gx', 'gy'), 'gz'), may hold values from -6 to 6
- w_up: bfloat16 [6144, 49152], P('gz', ('gx', 'gy')), may hold values from -0.078125 to 0.078125
- w_down: bfloat16 [49152, 6144], P(('gx', 'gy'), 'gz'), may hold values from -0.02734375 to 0.02734375
- cotangent: bfloat16 [24, 6144], P(('gx', 'gy'), 'gz'), may hold values from -6 to 6
Outputs:
- grad_in: float32 [24, 6144], P(('gx', 'gy'), 'gz')
- grad_up: bfloat16 [6144, 49152], P('gz', ('gx', 'gy'))
- grad_down: bfloat16 [49152, 6144], P(('gx', 'gy'), 'gz')
All inputs are finite; a program needn't handle non-finite values.
Results may differ from a plain program's by a relative error of at most 0.0049.
Values may be sent and summed in bfloat16 or wider, within the bound.
No kernel may reach another device: no remote copies, remote signals or barrier semaphores. Data moves between devices by JAX's collectives and lax.ppermute only.
A program may use at most 128 MiB of HBM per device.

v0:
```python
import math

import jax
import jax.numpy as jnp
from jax import lax
from jax.sharding import PartitionSpec as P

GELU_SCALE = math.sqrt(2.0 / math.pi)
CUBIC_COEFF = 0.044715


def activate(pre_act, back_grad):
    squared = pre_act * pre_act
    tangent = jnp.tanh(GELU_SCALE * pre_act * (1.0 + CUBIC_COEFF * squared))
    hidden = (0.5 * pre_act * (1.0 + tangent)).astype(jnp.bfloat16)
    gelu_slope = 0.5 * (1.0 + tangent) + 0.5 * pre_act * (1.0 - tangent * tangent) * GELU_SCALE * (
        1.0 + 3.0 * CUBIC_COEFF * squared
    )
    return (hidden, (back_grad * gelu_slope).astype(jnp.bfloat16))


def on_device(tokens, w_up, w_down, cotangent):
    rows_all, cot_all = (
        lax.all_gather(tokens, ("gx", "gy"), axis=0, tiled=True),
        lax.all_gather(cotangent, ("gx", "gy"), axis=0, tiled=True),
    )
    pre_part = jnp.dot(rows_all, w_up, preferred_element_type=jnp.float32)
    back_part = jnp.einsum("td,fd->tf", cot_all, w_down, preferred_element_type=jnp.float32)
    pre_act, back_grad = lax.psum((pre_part, back_part), "gz")
    hidden, pre_grad = activate(pre_act, back_grad)
    grad_up = jnp.einsum(
        "td,tf->df", rows_all, pre_grad, preferred_element_type=jnp.float32
    ).astype(jnp.bfloat16)
    grad_down = jnp.einsum("tf,td->fd", hidden, cot_all, preferred_element_type=jnp.float32).astype(
        jnp.bfloat16
    )
    grad_in = lax.psum_scatter(
        jnp.einsum("tf,df->td", pre_grad, w_up, preferred_element_type=jnp.float32),
        ("gx", "gy"),
        scatter_dimension=0,
        tiled=True,
    )
    return (grad_in, grad_up, grad_down)


def solution(mesh):
    placed = (
        P(("gx", "gy"), "gz"),
        P("gz", ("gx", "gy")),
        P(("gx", "gy"), "gz"),
        P(("gx", "gy"), "gz"),
    )
    return jax.shard_map(
        on_device,
        mesh=mesh,
        in_specs=placed,
        out_specs=(P(("gx", "gy"), "gz"), P("gz", ("gx", "gy")), P(("gx", "gy"), "gz")),
        check_vma=False,
    )
```

profile of v0, /device:TPU:24, one launch (start us, length us, event | category | flops | bytes accessed | tf_op | source)
XLA Modules:
  0.0 200.9 jit_solution(16386887218763422882)
XLA Ops:
  7.2 0.0 all-reduce.7.cloned.1.call-start
  7.2 15.9 %all-gather = bf16[8,3,1536]{2,1,0:T(4,128)(2,1)S(1)} all-gather(bf16[1,3,1536]{2,1,0:T(4,128)(2,1)} %bitcast.14), channel_id=1, replica_groups=mesh['gx'=4,'gy'=2,'gz'=4] {'gx','gy'}, dimensions={0}, use_global_device_ids=true | all-gather | bytes 82944 | tf_op jit(solution)/shard_map/all_gather | solution.py:25
  23.1 0.1 reshape.7
  23.2 15.6 %all-gather.1 = bf16[8,3,1536]{2,1,0:T(4,128)(2,1)S(1)} all-gather(bf16[1,3,1536]{2,1,0:T(4,128)(2,1)} %bitcast.15), channel_id=1, replica_groups=mesh['gx'=4,'gy'=2,'gz'=4] {'gx','gy'}, dimensions={0}, use_global_device_ids=true | all-gather | bytes 82944 | tf_op jit(solution)/shard_map/all_gather | solution.py:24
  38.8 0.1 reshape.9
  38.9 0.0 copy-start.2
  38.9 12.2 %fusion.9 = f32[24,6144]{1,0:T(8,128)} fusion(bf16[24,1536]{1,0:T(8,128)(2,1)S(1)} %reshape.7, bf16[6144,1536]{1,0:T(8,128)(2,1)} %param.6), kind=kOutput, calls=%fused_computation.15 | convolution fusion | flops 452984832 | bytes 19537920 | tf_op jit(solution)/shard_map/td,fd->tf/dot_general | solution.py:28
  51.0 9.7 %fusion.10 = f32[24,6144]{1,0:T(8,128)} fusion(bf16[24,1536]{1,0:T(8,128)(2,1)S(1)} %reshape.9, bf16[1536,6144]{1,0:T(8,128)(2,1)} %param.5), kind=kOutput, calls=%fused_computation.16 | convolution fusion | flops 452984832 | bytes 19537920 | tf_op jit(solution)/shard_map/dot_general | solution.py:27
  60.8 0.0 all-reduce.7.cloned.1.call-update
  60.8 0.2 all-reduce.5.cloned.1.call-start
  61.1 0.0 copy-done.2
  61.1 0.6 dynamic-slice
  62.3 54.1 %all-reduce.7.cloned.1.call-done = (f32[24,6144]{1,0:T(8,128)}, f32[24,6144]{1,0:T(8,128)}) async-done(((f32[24,6144]{1,0:T(8,128)}, f32[24,6144]{1,0:T(8,128)}), (f32[24,6144]{1,0:T(8,128)}, f32[24,6144]{1,0:T(8,128)})) %all-reduce.7.cloned.1.call-update) | async-done | bytes 1179664 | tf_op jit(solution)/shard_map/psum | solution.py:29
  116.4 0.0 copy-start
  116.4 0.0 copy-start.1
  116.4 10.7 %convolution_convert_fusion = bf16[6144,1536]{1,0:T(8,128)(2,1)} fusion(bf16[24,1536]{1,0:T(8,128)(2,1)S(1)} %reshape.7, f32[24,6144]{1,0:T(8,128)} %get-tuple-element.13), kind=kOutput, calls=%fused_computation | convolution fusion | flops 463749120 | bytes 19537920 | tf_op jit(solution)/shard_map/tf,td->fd/dot_general | solution.py:34
  127.1 0.0 copy-done
  127.1 0.0 copy-done.1
  127.1 0.4 multiply_convert_fusion.1
  127.5 12.0 %fusion.11 = f32[24,1536]{1,0:T(8,128)} fusion(bf16[24,6144]{1,0:T(8,128)(2,1)S(1)} %multiply_convert_fusion.1, bf16[1536,6144]{1,0:T(8,128)(2,1)} %param.5), kind=kOutput, calls=%fused_computation.17 | convolution fusion | flops 452984832 | bytes 19316736 | tf_op jit(solution)/shard_map/tf,df->td/dot_general | solution.py:38
  139.5 0.0 all-reduce.5.cloned.1.call-update
  139.5 9.2 %fusion = bf16[1536,6144]{0,1:T(8,128)(2,1)} fusion(bf16[24,6144]{1,0:T(8,128)(2,1)S(1)} %multiply_convert_fusion.1, bf16[24,1536]{1,0:T(8,128)(2,1)S(1)} %reshape.9), kind=kOutput, calls=%fused_computation.2 | convolution fusion | flops 462422016 | bytes 19243008 | tf_op jit(solution)/shard_map/td,tf->df/dot_general | solution.py:31
  148.7 24.6 %copy.9 = bf16[1536,6144]{1,0:T(8,128)(2,1)} copy(bf16[1536,6144]{0,1:T(8,128)(2,1)} %fusion) | data formatting | bytes 37748736
  173.3 19.2 %all-reduce.5.cloned.1.call-done = f32[24,1536]{1,0:T(8,128)} async-done(((f32[24,1536]{1,0:T(8,128)}), f32[24,1536]{1,0:T(8,128)}) %all-reduce.5.cloned.1.call-update) | async-done | bytes 147472
  192.5 1.5 constant_dynamic-slice_fusion
Async XLA Ops:
  7.2 109.2 %all-reduce.7.cloned.1.call-start = ((), (), s32[]{:S(2)}) async-start(), calls=%async_computation.1 | async-start | bytes 2359296 | tf_op jit(solution)/shard_map/psum | solution.py:29
  38.9 22.2 %copy-start.2 = (u32[32]{0:T(128)S(1)}, u32[32]{0:T(128)}, u32[]{:S(2)}) copy-start(u32[32]{0:T(128)} %constant.14) | copy-start | bytes 388
  60.8 131.7 %all-reduce.5.cloned.1.call-start = ((), (), s32[]{:S(2)}) async-start(), calls=%async_computation | async-start | bytes 294912
  116.4 10.7 %copy-start = (f32[24,6144]{1,0:T(8,128)S(1)}, f32[24,6144]{1,0:T(8,128)}, u32[]{:S(2)}) copy-start(f32[24,6144]{1,0:T(8,128)} %get-tuple-element.13) | copy-start | bytes 1769476
  116.4 10.7 %copy-start.1 = (f32[24,6144]{1,0:T(8,128)S(1)}, f32[24,6144]{1,0:T(8,128)}, u32[]{:S(2)}) copy-start(f32[24,6144]{1,0:T(8,128)} %get-tuple-element.12) | copy-start | bytes 1769476
Sparse Core Ops, SparseCore 0:
  60.9 55.4 all-reduce.6
  139.7 52.8 all-reduce.4
where the time goes:
time: 204 us; the launch traced here: 201 us
  waiting for transfers between devices  73.3 us (36%)
  matrix products  53.8 us (26%)
  blocking collectives  31.5 us (15%)
  local copies, waits for them, and re-layouts  26.8 us (13%)
  between operations  14.7 us (7%)
    psum x1, waiting for transfers between devices, on_device(): pre_act, back_grad = lax.psum((pre_part, back_part), 'gz')  54.1 us
    unnamed x11, local copies, waits for them, and re-layouts  26.8 us
    unnamed x3, waiting for transfers between devices  19.2 us
    all_gather x1, blocking collectives, on_device(): lax.all_gather(cotangent, ('gx', 'gy'), axis=0, tiled=True)  15.9 us
    all_gather x1, blocking collectives, on_device(): lax.all_gather(tokens, ('gx', 'gy'), axis=0, tiled=True)  15.6 us
    dot_general x1, matrix products, on_device(): jnp.einsum('td,fd->tf', cot_all, w_down, preferred_element_type=jnp.float32)  12.2 us
    dot_general x1, matrix products, on_device(): jnp.einsum('tf,df->td', pre_grad, w_up, preferred_element_type=jnp.float32)  12 us
    dot_general x1, matrix products, on_device(): jnp.einsum('tf,td->fd', hidden, cot_all, preferred_element_type=jnp.float32)  10.7 us
  transfers between devices with their start and end apart: 2, of which 2 were waited for; matrix products, arithmetic and copies ran while one was open for 17% of the time, Pallas kernels for 0%

commit v1 on v0

v1 whole, which is shorter than its diff:
```python
import functools
import math

import jax
import jax.numpy as jnp
from jax import lax
from jax.experimental import pallas as pl
from jax.experimental.pallas import tpu as pltpu
from jax.sharding import PartitionSpec as P

GELU_SCALE = math.sqrt(2.0 / math.pi)
CUBIC_COEFF = 0.044715
BF16 = jnp.bfloat16
F32 = jnp.float32
MIB = 1 << 20
PIECE = 512
SLAB = 256
STRIPES = 2
SMALL = 8 * MIB


def gelu(pre_act):
    squared = pre_act * pre_act
    tangent = jnp.tanh(GELU_SCALE * pre_act * (1.0 + CUBIC_COEFF * squared))
    hidden = (0.5 * pre_act * (1.0 + tangent)).astype(BF16)
    gelu_slope = 0.5 * (1.0 + tangent) + 0.5 * pre_act * (1.0 - tangent * tangent) * GELU_SCALE * (
        1.0 + 3.0 * CUBIC_COEFF * squared
    )
    return hidden, gelu_slope


def activate(pre_act, back_grad):
    hidden, gelu_slope = gelu(pre_act)
    return (hidden, (back_grad * gelu_slope).astype(BF16))


def plain(tokens, w_up, w_down, cotangent):
    rows_all, cot_all = (
        lax.all_gather(tokens, ("gx", "gy"), axis=0, tiled=True),
        lax.all_gather(cotangent, ("gx", "gy"), axis=0, tiled=True),
    )
    pre_part = jnp.dot(rows_all, w_up, preferred_element_type=F32)
    back_part = jnp.einsum("td,fd->tf", cot_all, w_down, preferred_element_type=F32)
    pre_act, back_grad = lax.psum((pre_part, back_part), "gz")
    hidden, pre_grad = activate(pre_act, back_grad)
    grad_up = jnp.einsum("td,tf->df", rows_all, pre_grad, preferred_element_type=F32).astype(BF16)
    grad_down = jnp.einsum("tf,td->fd", hidden, cot_all, preferred_element_type=F32).astype(BF16)
    grad_in = lax.psum_scatter(
        jnp.einsum("tf,df->td", pre_grad, w_up, preferred_element_type=F32),
        ("gx", "gy"),
        scatter_dimension=0,
        tiled=True,
    )
    return (grad_in, grad_up, grad_down)


def swap(value, axes, size, at):
    return lax.ppermute(value, axes, [(i, i ^ at) for i in range(size)])


def product(a, b, dims):
    return lax.dot_general(a, b, ((dims[:1], dims[1:]), ((), ())), preferred_element_type=F32)


def turn(block):
    return block.astype(F32).T.astype(BF16)


def in_vmem(count=1):
    return [pl.BlockSpec(memory_space=pltpu.VMEM)] * count


def anywhere(count=1):
    return [pl.BlockSpec(memory_space=pl.ANY)] * count


def keep_in(memory, value):
    return pltpu.with_memory_space_constraint(value, memory)


def cost(flops, bytes_accessed):
    return pl.CostEstimate(flops=flops, bytes_accessed=bytes_accessed, transcendentals=0)


def first_unit(other, quarter, size):
    return pl.multiple_of((((lax.axis_index("gz") & 1) ^ other) * 2 + quarter) * size, size)


def join_kernel(tokens_ref, cot_ref, out_ref, sems):
    copies = [
        pltpu.make_async_copy(from_ref, out_ref.at[i], sems.at[i]) for i, from_ref in enumerate((tokens_ref, cot_ref))
    ]
    for copy in copies:
        copy.start()
    for copy in copies:
        copy.wait()


def join(tokens, cotangent):
    return pl.pallas_call(
        join_kernel,
        in_specs=anywhere(2),
        out_specs=in_vmem()[0],
        out_shape=jax.ShapeDtypeStruct((2,) + tokens.shape, BF16),
        scratch_shapes=[pltpu.SemaphoreType.DMA((2,))],
        compiler_params=pltpu.CompilerParams(vmem_limit_bytes=SMALL),
        name="join",
    )(keep_in(pltpu.HBM, tokens), keep_in(pltpu.HBM, cotangent))


def pack_kernel(*refs):
    *block_refs, out_ref = refs
    for at, block_ref in enumerate(block_refs):
        out_ref[at] = block_ref[...]


def pack(blocks):
    return pl.pallas_call(
        pack_kernel,
        in_specs=in_vmem(len(blocks)),
        out_specs=in_vmem()[0],
        out_shape=jax.ShapeDtypeStruct((len(blocks),) + blocks[0].shape, BF16),
        compiler_params=pltpu.CompilerParams(vmem_limit_bytes=SMALL),
        name="pack",
    )(*blocks)


def unpack_kernel(*refs):
    *group_refs, rows_ref, cot_ref, turned_ref, wide = refs
    count, _, own, _ = group_refs[0].shape
    for i, out_ref in enumerate((rows_ref, cot_ref)):
        for to, (at, group_ref) in enumerate((at, x) for x in group_refs for at in range(count)):
            wide[i, to * own : (to + 1) * own] = group_ref[at, i].astype(F32)
        out_ref[...] = wide[i].astype(BF16)
    turned_ref[...] = turn(wide[0])


def unpack(groups):
    count, _, own, width = groups[0].shape
    tokens = own * count * len(groups)
    return pl.pallas_call(
        unpack_kernel,
        in_specs=in_vmem(len(groups)),
        out_specs=in_vmem(3),
        out_shape=[jax.ShapeDtypeStruct((tokens, width), BF16)] * 2 + [jax.ShapeDtypeStruct((width, tokens), BF16)],
        scratch_shapes=[pltpu.VMEM((2, tokens, width), F32)],
        compiler_params=pltpu.CompilerParams(vmem_limit_bytes=SMALL),
        name="unpack",
    )(*groups)


def add_up_kernel(*refs):
    *part_refs, out_ref = refs
    out_ref[...] = sum(part_ref[...].astype(F32) for part_ref in part_refs)


def add_up(parts):
    return pl.pallas_call(
        add_up_kernel,
        in_specs=in_vmem(len(parts)),
        out_specs=in_vmem()[0],
        out_shape=jax.ShapeDtypeStruct(parts[0].shape, F32),
        compiler_params=pltpu.CompilerParams(vmem_limit_bytes=SMALL),
        name="add_up",
    )(*parts)


class Copies:
    def __init__(self, from_ref, to_ref, sems):
        stripe = PIECE // STRIPES
        rows = [pl.ds(top, stripe) for top in range(0, to_ref.shape[0], stripe)]
        self.copies = [
            pltpu.make_async_copy(from_ref.at[at], to_ref.at[at], sems.at[i]) for i, at in enumerate(rows)
        ]

    def start(self):
        for copy in self.copies:
            copy.start()

    def wait(self):
        for copy in self.copies:
            copy.wait()


def up_copies(base, size, from_ref, to_ref, sems):
    columns, rows = pl.ds(base, size), range(0, to_ref.shape[0], PIECE)
    return [
        Copies(from_ref.at[pl.ds(top, PIECE), columns], to_ref.at[pl.ds(top, PIECE)], sems.at[i])
        for i, top in enumerate(rows)
    ]


def down_copies(base, size, from_ref, to_ref, sems):
    return [
        Copies(from_ref.at[pl.ds(base + top, PIECE)], to_ref.at[pl.ds(top, PIECE)], sems.at[i])
        for i, top in enumerate(range(0, size, PIECE))
    ]


def copy_sems(rows):
    return pltpu.SemaphoreType.DMA((rows // PIECE, STRIPES))


def load_kernel(other, quarter, up_ref, down_ref, _, up_kept, down_kept, up_sems, down_sems):
    size = up_kept.shape[1]
    base = first_unit(other, quarter, size)
    copies = up_copies(base, size, up_ref, up_kept, up_sems)
    copies += down_copies(base, size, down_ref, down_kept, down_sems)
    for copy in copies:
        copy.start()
    for copy in copies:
        copy.wait()


def load(w_up, w_down, other, quarter, after):
    width, units = w_up.shape
    size = units // 4
    return pl.pallas_call(
        functools.partial(load_kernel, other, quarter),
        in_specs=anywhere(3),
        out_specs=in_vmem(2),
        out_shape=[pltpu.VMEM((width, size), BF16), pltpu.VMEM((size, width), BF16)],
        scratch_shapes=[copy_sems(width), copy_sems(size)],
        compiler_params=pltpu.CompilerParams(vmem_limit_bytes=SMALL),
        cost_estimate=cost(0, 4 * width * size),
        name="load",
    )(keep_in(pltpu.HBM, w_up), keep_in(pltpu.HBM, w_down), after)


def multiply(rows_ref, cot_ref, up_buf, down_buf, out_ref, up_arriving=(), down_arriving=()):
    pre_act = None
    for i in range(up_buf.shape[0] // PIECE):
        piece = slice(i * PIECE, (i + 1) * PIECE)
        if up_arriving:
            up_arriving[i].wait()
        part = product(rows_ref[:, piece], up_buf[piece], (1, 0))
        pre_act = part if pre_act is None else pre_act + part
        if down_arriving:
            down_arriving[i].wait()
        out_ref[1, :, piece] = product(cot_ref[...], down_buf[piece], (1, 1)).astype(out_ref.dtype)
    out_ref[0] = pre_act.astype(out_ref.dtype)


def forward_other_kernel(rows_ref, cot_ref, up_first, down_first, up_ref, down_ref, *refs):
    first_out, second_out, up_kept, down_buf, *sems = refs
    size = up_kept.shape[1]
    base = first_unit(1, 1, size)
    ups = up_copies(base, size, up_ref, up_kept, sems[0])
    downs = down_copies(base, size, down_ref, down_buf, sems[1])
    for pair in zip(ups, downs):
        for copy in pair:
            copy.start()
    multiply(rows_ref, cot_ref, up_first, down_first, first_out)
    multiply(rows_ref, cot_ref, up_kept, down_buf, second_out, ups, downs)


def forward_other(rows, cot, up_first, down_first, w_up, w_down):
    tokens, width = rows.shape
    size = up_first.shape[1]
    return pl.pallas_call(
        forward_other_kernel,
        in_specs=in_vmem(4) + anywhere(2),
        out_specs=in_vmem(3),
        out_shape=[jax.ShapeDtypeStruct((2, tokens, size), BF16)] * 2 + [pltpu.VMEM((width, size), BF16)],
        scratch_shapes=[pltpu.VMEM((size, width), BF16), copy_sems(width), copy_sems(size)],
        compiler_params=pltpu.CompilerParams(vmem_limit_bytes=12 * MIB),
        cost_estimate=cost(8 * tokens * width * size, 4 * width * size),
        name="forward_other",
    )(
        rows,
        cot,
        keep_in(pltpu.VMEM, up_first),
        keep_in(pltpu.VMEM, down_first),
        keep_in(pltpu.HBM, w_up),
        keep_in(pltpu.HBM, w_down),
    )


def forward_own_kernel(quarter, rows_ref, cot_ref, up_ref, down_ref, *refs):
    out_ref, up_kept, down_buf, *sems = refs[-5:]
    size = up_kept.shape[1]
    base = first_unit(0, quarter, size)
    ups = up_copies(base, size, up_ref, up_kept, sems[0])
    downs = down_copies(base, size, down_ref, down_buf, sems[1])
    for pair in zip(ups, downs):
        for copy in pair:
            copy.start()
    multiply(rows_ref, cot_ref, up_kept, down_buf, out_ref, ups, downs)


def forward_own(rows, cot, w_up, w_down, quarter, after):
    tokens, width = rows.shape
    size = w_up.shape[1] // 4
    return pl.pallas_call(
        functools.partial(forward_own_kernel, quarter),
        in_specs=in_vmem(2) + anywhere(2 + len(after)),
        out_specs=in_vmem(2),
        out_shape=[jax.ShapeDtypeStruct((2, tokens, size), F32), pltpu.VMEM((width, size), BF16)],
        scratch_shapes=[pltpu.VMEM((size, width), BF16), copy_sems(width), copy_sems(size)],
        compiler_params=pltpu.CompilerParams(vmem_limit_bytes=12 * MIB),
        cost_estimate=cost(4 * tokens * width * size, 4 * width * size),
        name="forward_own",
    )(rows, cot, keep_in(pltpu.HBM, w_up), keep_in(pltpu.HBM, w_down), *after)


def activate_kernel(sums_ref, arrived_ref, *refs):
    sums = sums_ref[...] + arrived_ref[...].astype(F32)
    refs[-1][0], refs[-1][1] = activate(sums[0], sums[1])


def activated(sums, arrived, after):
    return pl.pallas_call(
        activate_kernel,
        in_specs=in_vmem(2) + anywhere(len(after)),
        out_specs=in_vmem()[0],
        out_shape=jax.ShapeDtypeStruct(sums.shape, BF16),
        compiler_params=pltpu.CompilerParams(vmem_limit_bytes=SMALL),
        name="activate",
    )(sums, arrived, *after)


def grad_in_sum(acts_ref, up_ref, turned):
    turned[...] = turn(acts_ref[1])
    return product(up_ref[...], turned[...], (1, 0)).T


def grads_kernel(places, shared, started, turned_ref, cot_ref, *refs):
    acts_refs, refs = refs[: len(places)], refs[len(places) :]
    up_refs, refs = refs[: len(places) * shared], refs[len(places) * shared :]
    again = shared and not started
    outs, scratch = refs[-8 - shared - again : -6], refs[-6:]
    up_out, down_out = outs[:2]
    if again:
        outs[3][...] = acts_refs[0][...]
    up_slots, down_slots, turned_hidden, turned_grad, up_sems, down_sems = scratch
    copies = []
    for place, (acts_ref, (other, quarter)) in enumerate(zip(acts_refs, places)):
        size = acts_ref.shape[2]
        base = first_unit(other, quarter, size)
        units = pl.ds(base, size)
        for i in range(size // SLAB):
            rows, slot = pl.ds(i * SLAB, SLAB), place * (size // SLAB) + i
            if i * SLAB % PIECE == 0:
                piece = slice(i * SLAB, i * SLAB + PIECE)
                turned_hidden[place, piece] = turn(acts_ref[0, :, piece])
            down_slots[slot] = product(turned_hidden[place, rows], cot_ref[...], (1, 0)).astype(BF16)
            to_ref = down_out.at[pl.ds(base + i * SLAB, SLAB)]
            copies.append(pltpu.make_async_copy(down_slots.at[slot], to_ref, down_sems.at[slot]))
            copies[-1].start()
        for i in range(turned_ref.shape[0] // SLAB):
            rows, slot = pl.ds(i * SLAB, SLAB), place * (turned_ref.shape[0] // SLAB) + i
            up_slots[slot] = product(turned_ref[rows], acts_ref[1], (1, 0)).astype(BF16)
            copies.append(pltpu.make_async_copy(up_slots.at[slot], up_out.at[rows, units], up_sems.at[slot]))
            copies[-1].start()
    if shared:
        total = refs[0][...] if started else None
        for place, (acts_ref, up_ref) in enumerate(zip(acts_refs, up_refs)):
            part = grad_in_sum(acts_ref, up_ref, turned_grad.at[place])
            total = part if total is None else total + part
        outs[2][...] = total
    for copy in copies:
        copy.wait()


def grads(turned, cot, units, places, acts, up_quarters=(), total=None, so_far=(), after=()):
    tokens, width = cot.shape
    size = acts[0].shape[2]
    ups, downs = (len(places) * x // SLAB for x in (width, size))
    shared = bool(up_quarters)
    totals = () if total is None else (total,)
    again = shared and not totals
    before = 2 + len(acts) + len(up_quarters) + len(totals)
    return pl.pallas_call(
        functools.partial(grads_kernel, places, shared, bool(totals)),
        in_specs=in_vmem(before) + anywhere(len(so_far) + len(after)),
        out_specs=anywhere(2) + in_vmem(shared + again),
        out_shape=[jax.ShapeDtypeStruct((width, units), BF16), jax.ShapeDtypeStruct((units, width), BF16)]
        + [jax.ShapeDtypeStruct((tokens, width), F32)] * shared
        + [jax.ShapeDtypeStruct(acts[0].shape, BF16)] * again,
        scratch_shapes=[
            pltpu.VMEM((ups, SLAB, size), BF16),
            pltpu.VMEM((downs, SLAB, width), BF16),
            pltpu.VMEM((len(places), size, tokens), BF16),
            pltpu.VMEM((len(places), size, tokens), BF16),
            pltpu.SemaphoreType.DMA((ups,)),
            pltpu.SemaphoreType.DMA((downs,)),
        ],
        input_output_aliases={before: 0, before + 1: 1} if so_far else {},
        compiler_params=pltpu.CompilerParams(vmem_limit_bytes=(4 + 12 * len(places)) * MIB),
        cost_estimate=cost(6 * tokens * width * size * len(places), 4 * width * size * len(places)),
        name="grads",
    )(turned, cot, *acts, *(keep_in(pltpu.VMEM, x) for x in up_quarters), *totals, *so_far, *after)


def grad_in_kernel(total_ref, acts_ref, up_ref, *out_refs):
    total = total_ref[...] + product(acts_ref[1], up_ref[...], (1, 1))
    count, own, _ = out_refs[0].shape
    for i in range(count * len(out_refs)):
        out_refs[i % len(out_refs)][i // len(out_refs)] = total[i * own : (i + 1) * own].astype(BF16)


def grad_in_parts(total, acts, up_quarter, cores, chips):
    tokens, width = total.shape
    size = acts.shape[2]
    return pl.pallas_call(
        grad_in_kernel,
        in_specs=in_vmem(3),
        out_specs=in_vmem(cores),
        out_shape=[jax.ShapeDtypeStruct((chips, tokens // chips // cores, width), BF16)] * cores,
        compiler_params=pltpu.CompilerParams(vmem_limit_bytes=SMALL),
        cost_estimate=cost(2 * tokens * width * size, 2 * width * size),
        name="grad_in",
    )(total, acts, keep_in(pltpu.VMEM, up_quarter))


def split_by_chip_kernel(*refs):
    chips = refs[0].shape[0]
    part_refs, out_refs = refs[:-chips], refs[-chips:]
    total = sum(part_ref[...].astype(F32) for part_ref in part_refs)
    for i, out_ref in enumerate(out_refs):
        out_ref[...] = total[i].astype(out_ref.dtype)


def split_by_chip(parts):
    chips, own, width = parts[0].shape
    return pl.pallas_call(
        split_by_chip_kernel,
        in_specs=in_vmem(len(parts)),
        out_specs=in_vmem(chips),
        out_shape=[jax.ShapeDtypeStruct((own, width), F32 if i == 0 else BF16) for i in range(chips)],
        compiler_params=pltpu.CompilerParams(vmem_limit_bytes=SMALL),
        name="split_by_chip",
    )(*parts)


def pair_sums_kernel(own_ref, arrived_ref, *refs):
    sums_ref, sent_ref = refs[-2:]
    sums = own_ref[...] + arrived_ref[...].astype(F32)
    sums_ref[...], sent_ref[...] = sums, sums.astype(BF16)


def pair_sums(own, arrived, after=()):
    return pl.pallas_call(
        pair_sums_kernel,
        in_specs=in_vmem(2) + anywhere(len(after)),
        out_specs=in_vmem(2),
        out_shape=[jax.ShapeDtypeStruct(own.shape, F32), jax.ShapeDtypeStruct(own.shape, BF16)],
        compiler_params=pltpu.CompilerParams(vmem_limit_bytes=SMALL),
        name="pair_sums",
    )(own, arrived, *after)


def split_plan(owners, splits, tokens, w_up, w_down, cotangent):
    group = ("gx", "gy")
    units = w_up.shape[1]
    core, chips = 2 % owners, [at for at in range(owners) if not at & 2]
    both = join(tokens, cotangent)
    both = pack([both, swap(both, group, owners, core)] if core else [both])
    kept, parts, sums, acts = {}, {}, {}, {}
    kept[1, 0], down_first = load(w_up, w_down, 1, 0, after=both)
    rows, cot, turned = unpack([both] + [swap(both, group, owners, at) for at in chips[1:]])

    parts[1, 0], parts[1, 1], kept[1, 1] = forward_other(rows, cot, kept[1, 0], down_first, w_up, w_down)
    theirs = [swap(parts[1, quarter], "gz", splits, 1) for quarter in (0, 1)]
    parts[0, 0], kept[0, 0] = forward_own(rows, cot, w_up, w_down, 0, after=(parts[1, 0],))
    sums[0], sent = pair_sums(parts[0, 0], theirs[0])
    arrived = swap(sent, "gz", splits, 2)
    parts[0, 1], kept[0, 1] = forward_own(rows, cot, w_up, w_down, 1, after=(sent, theirs[1]))
    sums[1], sent = pair_sums(parts[0, 1], theirs[1])
    late = swap(sent, "gz", splits, 2)

    acts[0, 0] = activated(sums[0], arrived, after=(sent,))
    *grad_arrays, total, again = grads(turned, cot, units, [(0, 0)], [acts[0, 0]], [kept[0, 0]])
    acts[1, 0] = swap(again, "gz", splits, 1)
    acts[0, 1] = activated(sums[1], late, after=(total,))
    acts[1, 1] = swap(acts[0, 1], "gz", splits, 1)
    for place in [(0, 1), (1, 0)]:
        *grad_arrays, total = grads(turned, cot, units, [place], [acts[place]], [kept[place]], total, grad_arrays)
    by_core = grad_in_parts(total, acts[1, 1], kept[1, 1], 2 if core else 1, len(chips))
    by_core = [by_core[0]] + [swap(x, group, owners, core) for x in by_core[1:]]
    by_chip = split_by_chip(by_core)
    grad_up, grad_down = grads(
        turned, cot, units, [(1, 1)], [acts[1, 1]], so_far=grad_arrays, after=(by_chip[0],)
    )
    grad_in = add_up([by_chip[0]] + [swap(x, group, owners, at) for x, at in zip(by_chip[1:], chips[1:])])
    return (grad_in, grad_up, grad_down)


def solution(mesh):
    owners, splits = mesh.shape["gx"] * mesh.shape["gy"], mesh.shape["gz"]

    def on_device(tokens, w_up, w_down, cotangent):
        if w_up.shape[1] % (4 * PIECE) or w_up.shape[0] % PIECE or owners > 8 or splits != 4:
            return plain(tokens, w_up, w_down, cotangent)
        return split_plan(owners, splits, tokens, w_up, w_down, cotangent)

    placed = (
        P(("gx", "gy"), "gz"),
        P("gz", ("gx", "gy")),
        P(("gx", "gy"), "gz"),
        P(("gx", "gy"), "gz"),
    )
    return jax.shard_map(
        on_device,
        mesh=mesh,
        in_specs=placed,
        out_specs=(P(("gx", "gy"), "gz"), P("gz", ("gx", "gy")), P(("gx", "gy"), "gz")),
        check_vma=False,
    )
```

time: 204 us -> 63 us (0.31); the launches traced: 201 us -> 62.7 us
  waiting for transfers between devices: 73.3 us -> 7.92 us
  matrix products: 53.8 us -> 0 us
  Pallas kernels: 0 us -> 39.9 us
  blocking collectives: 31.5 us -> 0 us
  local copies, waits for them, and re-layouts: 26.8 us -> 0 us
  between operations: 14.7 us -> 0.86 us
  starting transfers between devices: 0.26 us -> 14 us
    psum x1 -> x0, waiting for transfers between devices: 54.1 us -> none  [on_device(): pre_act, back_grad = lax.psum((pre_part, back_part), 'gz')]
    dot_general x5 -> x0, matrix products: 53.8 us -> none  [the longest x1 12.2 us: on_device(): jnp.einsum('td,fd->tf', cot_all, w_down, preferred_element_type=jnp.float32)]
    pallas_call x0 -> x18, Pallas kernels: none -> 39.9 us  [the longest x4 16.7 us: grads(): pl.pallas_call(functools.partial(grads_kernel, places, shared, bool(total...]
    all_gather x2 -> x0, blocking collectives: 31.5 us -> none  [the longest x1 15.9 us: on_device(): lax.all_gather(cotangent, ('gx', 'gy'), axis=0, tiled=True)]
    unnamed x11 -> x0, local copies, waits for them, and re-layouts: 26.8 us -> none
    unnamed x3 -> x0, waiting for transfers between devices: 19.2 us -> none
    ppermute x0 -> x14, starting transfers between devices: none -> 14 us  [swap(): return lax.ppermute(value, axes, [(i, i ^ at) for i in range(size)])]
    ppermute x0 -> x14, waiting for transfers between devices: none -> 7.92 us  [swap(): return lax.ppermute(value, axes, [(i, i ^ at) for i in range(size)])]
  transfers between devices with their start and end apart: 2 -> 14, of which waited for: 2 -> 5; matrix products, arithmetic and copies ran while one was open for 17% -> 0% of each run, Pallas kernels for 0% -> 48%
where the time goes in v1:
time: 63 us; the launch traced here: 62.7 us
  Pallas kernels  39.9 us (63%)
  starting transfers between devices  14 us (22%)
  waiting for transfers between devices  7.92 us (13%)
  between operations  0.86 us (1%)
    pallas_call x4, Pallas kernels, grads(): pl.pallas_call(functools.partial(grads_kernel, places, shared, bool(total...  16.7 us
    ppermute x14, starting transfers between devices, swap(): return lax.ppermute(value, axes, [(i, i ^ at) for i in range(size)])  14 us
    pallas_call x2, Pallas kernels, forward_own(): pl.pallas_call(functools.partial(forward_own_kernel, quarter), in_specs=i...  9.14 us
    ppermute x14, waiting for transfers between devices, swap(): return lax.ppermute(value, axes, [(i, i ^ at) for i in range(size)])  7.92 us
    pallas_call x1, Pallas kernels, forward_other(): pl.pallas_call(forward_other_kernel, in_specs=in_vmem(4) + anywhere(2), o...  6.82 us
    pallas_call x1, Pallas kernels, load(): pl.pallas_call(functools.partial(load_kernel, other, quarter), in_specs=a...  3.8 us
    pallas_call x1, Pallas kernels, grad_in_parts(): pl.pallas_call(grad_in_kernel, in_specs=in_vmem(3), out_specs=in_vmem(cor...  1.49 us
  transfers between devices with their start and end apart: 14, of which 5 were waited for; matrix products, arithmetic and copies ran while one was open for 0% of the time, Pallas kernels for 48%

profile of v1, /device:TPU:24, one launch (start us, length us, event | category | flops | bytes accessed | tf_op | source)
XLA Modules:
  0.0 62.7 jit_solution(13635966111758894332)
XLA Ops:
  0.6 0.7 %join.1.refs_0_ = bf16[2,3,1536]{2,1,0:T(4,128)(2,1)S(1)} custom-call(bf16[3,1536]{1,0:T(4,128)(2,1)} %tokens_ref.1, bf16[3,1536]{1,0:T(4,128)(2,1)} %cot_ref.1), custom_call_target="tpu_custom_call" | custom-call | tf_op jit(solution)/shard_map/join/pallas_call | solution.py:100
  1.4 0.1 collective-permute-start
  1.5 1.2 %collective-permute-done.refs_1_ = bf16[2,3,1536]{2,1,0:T(4,128)(2,1)S(1)} collective-permute-done((bf16[2,3,1536]{2,1,0:T(4,128)(2,1)S(1)}, bf16[2,3,1536]{2,1,0:T(4,128)(2,1)S(1)}, u32[]{:S(2)}, u32[]{:S(2)}) %collective-permute-start) | collective-permute-done | bytes 18464 | tf_op jit(solution)/shard_map/ppermute | solution.py:58
  2.7 1.6 %collective-permute-start.1 = (bf16[2,2,3,1536]{3,2,1,0:T(4,128)(2,1)S(1)}, bf16[2,2,3,1536]{3,2,1,0:T(4,128)(2,1)S(1)}, u32[]{:S(2)}, u32[]{:S(2)}) collective-permute-start(bf16[2,2,3,1536]{3,2,1,0:T(4,128)(2,1)S(1)} %pack.1.refs_0_._), channel_id=1, source_target_pairs={{0,4},{4,0},{8,12},{12,8},{16,20},{20,16},{24,28},{28,24},{1,5},{5... | collective-permute-start | bytes 110600 | tf_op jit(solution)/shard_map/ppermute | solution.py:58
  4.2 1.5 %collective-permute-start.2 = (bf16[2,2,3,1536]{3,2,1,0:T(4,128)(2,1)S(1)}, bf16[2,2,3,1536]{3,2,1,0:T(4,128)(2,1)S(1)}, u32[]{:S(2)}, u32[]{:S(2)}) collective-permute-start(bf16[2,2,3,1536]{3,2,1,0:T(4,128)(2,1)S(1)} %pack.1.refs_0_._), channel_id=1, source_target_pairs={{0,16},{4,20},{8,24},{12,28},{16,0},{20,4},{24,8},{28,12},{1,17},{... | collective-permute-start | bytes 110600 | tf_op jit(solution)/shard_map/ppermute | solution.py:58
  5.7 0.5 collective-permute-start.3
  6.2 3.8 %load.1 = (bf16[1536,1536]{1,0:T(8,128)(2,1)S(1)}, bf16[1536,1536]{1,0:T(8,128)(2,1)S(1)}) custom-call(bf16[1536,6144]{1,0:T(8,128)(2,1)} %up_ref.7, bf16[6144,1536]{1,0:T(8,128)(2,1)} %down_ref.7, bf16[2,2,3,1536]{3,2,1,0:T(4,128)(2,1)S(1)} %pack.1.refs_0_._), custom_call_target="tpu_custom_call" | custom-call | bytes 9437184 | tf_op jit(solution)/shard_map/load/pallas_call | solution.py:218
  10.0 0.7 %collective-permute-done.3.refs_3_ = bf16[2,2,3,1536]{3,2,1,0:T(4,128)(2,1)S(1)} collective-permute-done((bf16[2,2,3,1536]{3,2,1,0:T(4,128)(2,1)S(1)}, bf16[2,2,3,1536]{3,2,1,0:T(4,128)(2,1)S(1)}, u32[]{:S(2)}, u32[]{:S(2)}) %collective-permute-start.3) | collective-permute-done | bytes 36896 | tf_op jit(solution)/shard_map/ppermute | solution.py:58
  10.7 0.2 unpack.1
  11.0 6.8 %forward_other.1 = (bf16[2,24,1536]{2,1,0:T(8,128)(2,1)S(1)}, bf16[2,24,1536]{2,1,0:T(8,128)(2,1)S(1)}, bf16[1536,1536]{1,0:T(8,128)(2,1)S(1)}) custom-call(bf16[24,1536]{1,0:T(8,128)(2,1)S(1)} %get-tuple-element.39.rows_ref, bf16[24,1536]{1,0:T(8,128)(2,1)S(1)} %get-tuple-element.38.cot_ref, bf16[1536,1536]{1,0:T(8,128)(2,1)S(1)} %get-tuple-element.40.up_first.refs_1_, ...), custom_call_target="tpu_custom_call" | custom-call | flops 452984832 | bytes 9437184 | tf_op jit(solution)/shard_map/forward_other/pallas_call | solution.py:260
  17.8 0.5 collective-permute-start.4
  18.3 1.6 %collective-permute-start.6 = (bf16[2,24,1536]{2,1,0:T(8,128)(2,1)S(1)}, bf16[2,24,1536]{2,1,0:T(8,128)(2,1)S(1)}, u32[]{:S(2)}, u32[]{:S(2)}) collective-permute-start(bf16[2,24,1536]{2,1,0:T(8,128)(2,1)S(1)} %get-tuple-element.46), channel_id=1, source_target_pairs={{0,1},{1,0},{2,3},{3,2},{4,5},{5,4},{6,7},{7,6},{8,9},{9,8},{10,11... | collective-permute-start | bytes 442376 | tf_op jit(solution)/shard_map/ppermute | solution.py:58
  19.9 4.6 %forward_own.2 = (f32[2,24,1536]{2,1,0:T(8,128)S(1)}, bf16[1536,1536]{1,0:T(8,128)(2,1)S(1)}) custom-call(bf16[24,1536]{1,0:T(8,128)(2,1)S(1)} %get-tuple-element.39.rows_ref, bf16[24,1536]{1,0:T(8,128)(2,1)S(1)} %get-tuple-element.38.cot_ref, bf16[1536,6144]{1,0:T(8,128)(2,1)} %up_ref.7, bf16[6144,1536]{1,0:T(8,128)(2,1)} %down_ref.7, ...), custom_call_target="tpu_custom_call" | custom-call | flops 226492416 | bytes 9437184 | tf_op jit(solution)/shard_map/forward_own/pallas_call | solution.py:294
  24.5 0.4 collective-permute-start.5
  24.9 0.5 collective-permute-done.6.refs_1_.arrived_ref
  25.4 4.6 %forward_own.3 = (f32[2,24,1536]{2,1,0:T(8,128)S(1)}, bf16[1536,1536]{1,0:T(8,128)(2,1)S(1)}) custom-call(bf16[24,1536]{1,0:T(8,128)(2,1)S(1)} %get-tuple-element.39.rows_ref, bf16[24,1536]{1,0:T(8,128)(2,1)S(1)} %get-tuple-element.38.cot_ref, bf16[1536,6144]{1,0:T(8,128)(2,1)} %up_ref.7, bf16[6144,1536]{1,0:T(8,128)(2,1)} %down_ref.7, ...), custom_call_target="tpu_custom_call" | custom-call | flops 226492416 | bytes 9437184 | tf_op jit(solution)/shard_map/forward_own/pallas_call | solution.py:294
  30.0 2.2 %collective-permute-start.8 = (bf16[2,24,1536]{2,1,0:T(8,128)(2,1)S(1)}, bf16[2,24,1536]{2,1,0:T(8,128)(2,1)S(1)}, u32[]{:S(2)}, u32[]{:S(2)}) collective-permute-start(bf16[2,24,1536]{2,1,0:T(8,128)(2,1)S(1)} %get-tuple-element.48.refs_0_), channel_id=1, source_target_pairs={{0,2},{1,3},{2,0},{3,1},{4,6},{5,7},{6,4},{7,5},{8,10},{9,11},{10,... | collective-permute-start | bytes 442376 | tf_op jit(solution)/shard_map/ppermute | solution.py:58
  32.2 4.3 %collective-permute-done.5.arrived_ref = bf16[2,24,1536]{2,1,0:T(8,128)(2,1)S(1)} collective-permute-done((bf16[2,24,1536]{2,1,0:T(8,128)(2,1)S(1)}, bf16[2,24,1536]{2,1,0:T(8,128)(2,1)S(1)}, u32[]{:S(2)}, u32[]{:S(2)}) %collective-permute-start.5) | collective-permute-done | bytes 147488 | tf_op jit(solution)/shard_map/ppermute | solution.py:58
  36.5 0.1 activate.2.refs_0_
  36.6 4.1 %grads.4 = (bf16[1536,6144]{1,0:T(8,128)(2,1)}, bf16[6144,1536]{1,0:T(8,128)(2,1)}, f32[24,1536]{1,0:T(8,128)S(1)}, bf16[2,24,1536]{2,1,0:T(8,128)(2,1)S(1)}) custom-call(bf16[1536,24]{1,0:T(8,128)(2,1)S(1)} %get-tuple-element.37.turned_ref, bf16[24,1536]{1,0:T(8,128)(2,1)S(1)} %get-tuple-element.38.cot_ref, bf16[2,24,1536]{2,1,0:T(8,128)(2,1)S(1)} %activate.2.refs_0_, ...), custom_call_target="tpu_custom_call" | custom-call | flops 339738624 | bytes 9437184 | tf_op jit(solution)/shard_map/grads/pallas_call | solution.py:373
  40.8 0.1 collective-permute-start.7
  40.9 0.1 activate.3.refs_0_
  41.0 2.1 %collective-permute-start.9 = (bf16[2,24,1536]{2,1,0:T(8,128)(2,1)S(1)}, bf16[2,24,1536]{2,1,0:T(8,128)(2,1)S(1)}, u32[]{:S(2)}, u32[]{:S(2)}) collective-permute-start(bf16[2,24,1536]{2,1,0:T(8,128)(2,1)S(1)} %activate.3.refs_0_), channel_id=1, source_target_pairs={{0,1},{1,0},{2,3},{3,2},{4,5},{5,4},{6,7},{7,6},{8,9},{9,8},{10,11... | collective-permute-start | bytes 442376 | tf_op jit(solution)/shard_map/ppermute | solution.py:58
  43.1 4.3 %grads.5 = (bf16[1536,6144]{1,0:T(8,128)(2,1)}, bf16[6144,1536]{1,0:T(8,128)(2,1)}, f32[24,1536]{1,0:T(8,128)S(1)}) custom-call(bf16[1536,24]{1,0:T(8,128)(2,1)S(1)} %get-tuple-element.37.turned_ref, bf16[24,1536]{1,0:T(8,128)(2,1)S(1)} %get-tuple-element.38.cot_ref, ...), custom_call_target="tpu_custom_call", output_to_operand_aliasing={{0}: (5, {}), {1}: (6, {})} | custom-call | flops 339738624 | bytes 9437184 | tf_op jit(solution)/shard_map/grads/pallas_call | solution.py:373
  47.4 4.1 %grads.6 = (bf16[1536,6144]{1,0:T(8,128)(2,1)}, bf16[6144,1536]{1,0:T(8,128)(2,1)}, f32[24,1536]{1,0:T(8,128)S(1)}) custom-call(bf16[1536,24]{1,0:T(8,128)(2,1)S(1)} %get-tuple-element.37.turned_ref, bf16[24,1536]{1,0:T(8,128)(2,1)S(1)} %get-tuple-element.38.cot_ref, ...), custom_call_target="tpu_custom_call", output_to_operand_aliasing={{0}: (5, {}), {1}: (6, {})} | custom-call | flops 339738624 | bytes 9437184 | tf_op jit(solution)/shard_map/grads/pallas_call | solution.py:373
  51.5 1.5 %grad_in.1 = (bf16[4,3,1536]{2,1,0:T(4,128)(2,1)S(1)}, bf16[4,3,1536]{2,1,0:T(4,128)(2,1)S(1)}) custom-call(f32[24,1536]{1,0:T(8,128)S(1)} %get-tuple-element.59.total_ref, bf16[2,24,1536]{2,1,0:T(8,128)(2,1)S(1)} %collective-permute-done.9.acts_ref.refs_0_, bf16[1536,1536]{1,0:T(8,128)(2,1)S(1)} %get-tuple-element.60.up_ref), custom_call_target="tpu_custom_call" | custom-call | flops 113246208 | bytes 4718592 | tf_op jit(solution)/shard_map/grad_in/pallas_call | solution.py:405
  53.0 0.1 collective-permute-start.10
  53.1 1.2 %collective-permute-done.10.refs_1_ = bf16[4,3,1536]{2,1,0:T(4,128)(2,1)S(1)} collective-permute-done((bf16[4,3,1536]{2,1,0:T(4,128)(2,1)S(1)}, bf16[4,3,1536]{2,1,0:T(4,128)(2,1)S(1)}, u32[]{:S(2)}, u32[]{:S(2)}) %collective-permute-start.10) | collective-permute-done | bytes 36896 | tf_op jit(solution)/shard_map/ppermute | solution.py:58
  54.4 0.7 %collective-permute-start.12 = (bf16[3,1536]{1,0:T(4,128)(2,1)S(1)}, bf16[3,1536]{1,0:T(4,128)(2,1)S(1)}, u32[]{:S(2)}, u32[]{:S(2)}) collective-permute-start(bf16[3,1536]{1,0:T(4,128)(2,1)S(1)} %get-tuple-element.65), channel_id=1, source_target_pairs={{0,16},{4,20},{8,24},{12,28},{16,0},{20,4},{24,8},{28,12},{1,17},{... | collective-permute-start | bytes 27656 | tf_op jit(solution)/shard_map/ppermute | solution.py:58
  55.2 2.7 %collective-permute-start.13 = (bf16[3,1536]{1,0:T(4,128)(2,1)S(1)}, bf16[3,1536]{1,0:T(4,128)(2,1)S(1)}, u32[]{:S(2)}, u32[]{:S(2)}) collective-permute-start(bf16[3,1536]{1,0:T(4,128)(2,1)S(1)} %get-tuple-element.66), channel_id=1, source_target_pairs={{0,20},{4,16},{8,28},{12,24},{16,4},{20,0},{24,12},{28,8},{1,21},{... | collective-permute-start | bytes 27656 | tf_op jit(solution)/shard_map/ppermute | solution.py:58
  57.9 4.1 %grads.7 = (bf16[1536,6144]{1,0:T(8,128)(2,1)}, bf16[6144,1536]{1,0:T(8,128)(2,1)}) custom-call(bf16[1536,24]{1,0:T(8,128)(2,1)S(1)} %get-tuple-element.37.turned_ref, bf16[24,1536]{1,0:T(8,128)(2,1)S(1)} %get-tuple-element.38.cot_ref, ...), custom_call_target="tpu_custom_call", output_to_operand_aliasing={{0}: (3, {}), {1}: (4, {})} | custom-call | flops 339738624 | bytes 9437184 | tf_op jit(solution)/shard_map/grads/pallas_call | solution.py:373
  62.1 0.6 add_up.1
  (14 shorter events, 0.2 us)
Async XLA Ops:
  1.4 1.3 %collective-permute-start = (bf16[2,3,1536]{2,1,0:T(4,128)(2,1)S(1)}, bf16[2,3,1536]{2,1,0:T(4,128)(2,1)S(1)}, u32[]{:S(2)}, u32[]{:S(2)}) collective-permute-start(bf16[2,3,1536]{2,1,0:T(4,128)(2,1)S(1)} %join.1.refs_0_), channel_id=1, source_target_pairs={{0,8},{4,12},{8,0},{12,4},{16,24},{20,28},{24,16},{28,20},{1,9},{5... | collective-permute-start | bytes 55304 | tf_op jit(solution)/shard_map/ppermute | solution.py:58
  2.7 7.4 %collective-permute-start.1 = (bf16[2,2,3,1536]{3,2,1,0:T(4,128)(2,1)S(1)}, bf16[2,2,3,1536]{3,2,1,0:T(4,128)(2,1)S(1)}, u32[]{:S(2)}, u32[]{:S(2)}) collective-permute-start(bf16[2,2,3,1536]{3,2,1,0:T(4,128)(2,1)S(1)} %pack.1.refs_0_._), channel_id=1, source_target_pairs={{0,4},{4,0},{8,12},{12,8},{16,20},{20,16},{24,28},{28,24},{1,5},{5... | collective-permute-start | bytes 110600 | tf_op jit(solution)/shard_map/ppermute | solution.py:58
  4.2 5.8 %collective-permute-start.2 = (bf16[2,2,3,1536]{3,2,1,0:T(4,128)(2,1)S(1)}, bf16[2,2,3,1536]{3,2,1,0:T(4,128)(2,1)S(1)}, u32[]{:S(2)}, u32[]{:S(2)}) collective-permute-start(bf16[2,2,3,1536]{3,2,1,0:T(4,128)(2,1)S(1)} %pack.1.refs_0_._), channel_id=1, source_target_pairs={{0,16},{4,20},{8,24},{12,28},{16,0},{20,4},{24,8},{28,12},{1,17},{... | collective-permute-start | bytes 110600 | tf_op jit(solution)/shard_map/ppermute | solution.py:58
  5.7 5.0 %collective-permute-start.3 = (bf16[2,2,3,1536]{3,2,1,0:T(4,128)(2,1)S(1)}, bf16[2,2,3,1536]{3,2,1,0:T(4,128)(2,1)S(1)}, u32[]{:S(2)}, u32[]{:S(2)}) collective-permute-start(bf16[2,2,3,1536]{3,2,1,0:T(4,128)(2,1)S(1)} %pack.1.refs_0_._), channel_id=1, source_target_pairs={{0,20},{4,16},{8,28},{12,24},{16,4},{20,0},{24,12},{28,8},{1,21},{... | collective-permute-start | bytes 110600 | tf_op jit(solution)/shard_map/ppermute | solution.py:58
  17.8 6.7 %collective-permute-start.4 = (bf16[2,24,1536]{2,1,0:T(8,128)(2,1)S(1)}, bf16[2,24,1536]{2,1,0:T(8,128)(2,1)S(1)}, u32[]{:S(2)}, u32[]{:S(2)}) collective-permute-start(bf16[2,24,1536]{2,1,0:T(8,128)(2,1)S(1)} %get-tuple-element.42.refs_0_), channel_id=1, source_target_pairs={{0,1},{1,0},{2,3},{3,2},{4,5},{5,4},{6,7},{7,6},{8,9},{9,8},{10,11... | collective-permute-start | bytes 442376 | tf_op jit(solution)/shard_map/ppermute | solution.py:58
  18.3 7.1 %collective-permute-start.6 = (bf16[2,24,1536]{2,1,0:T(8,128)(2,1)S(1)}, bf16[2,24,1536]{2,1,0:T(8,128)(2,1)S(1)}, u32[]{:S(2)}, u32[]{:S(2)}) collective-permute-start(bf16[2,24,1536]{2,1,0:T(8,128)(2,1)S(1)} %get-tuple-element.46), channel_id=1, source_target_pairs={{0,1},{1,0},{2,3},{3,2},{4,5},{5,4},{6,7},{7,6},{8,9},{9,8},{10,11... | collective-permute-start | bytes 442376 | tf_op jit(solution)/shard_map/ppermute | solution.py:58
  24.5 12.0 %collective-permute-start.5 = (bf16[2,24,1536]{2,1,0:T(8,128)(2,1)S(1)}, bf16[2,24,1536]{2,1,0:T(8,128)(2,1)S(1)}, u32[]{:S(2)}, u32[]{:S(2)}) collective-permute-start(bf16[2,24,1536]{2,1,0:T(8,128)(2,1)S(1)} %get-tuple-element.45.refs_0_), channel_id=1, source_target_pairs={{0,2},{1,3},{2,0},{3,1},{4,6},{5,7},{6,4},{7,5},{8,10},{9,11},{10,... | collective-permute-start | bytes 442376 | tf_op jit(solution)/shard_map/ppermute | solution.py:58
  30.0 10.8 %collective-permute-start.8 = (bf16[2,24,1536]{2,1,0:T(8,128)(2,1)S(1)}, bf16[2,24,1536]{2,1,0:T(8,128)(2,1)S(1)}, u32[]{:S(2)}, u32[]{:S(2)}) collective-permute-start(bf16[2,24,1536]{2,1,0:T(8,128)(2,1)S(1)} %get-tuple-element.48.refs_0_), channel_id=1, source_target_pairs={{0,2},{1,3},{2,0},{3,1},{4,6},{5,7},{6,4},{7,5},{8,10},{9,11},{10,... | collective-permute-start | bytes 442376 | tf_op jit(solution)/shard_map/ppermute | solution.py:58
  40.8 6.6 %collective-permute-start.7 = (bf16[2,24,1536]{2,1,0:T(8,128)(2,1)S(1)}, bf16[2,24,1536]{2,1,0:T(8,128)(2,1)S(1)}, u32[]{:S(2)}, u32[]{:S(2)}) collective-permute-start(bf16[2,24,1536]{2,1,0:T(8,128)(2,1)S(1)} %get-tuple-element.50), channel_id=1, source_target_pairs={{0,1},{1,0},{2,3},{3,2},{4,5},{5,4},{6,7},{7,6},{8,9},{9,8},{10,11... | collective-permute-start | bytes 442376 | tf_op jit(solution)/shard_map/ppermute | solution.py:58
  41.0 10.5 %collective-permute-start.9 = (bf16[2,24,1536]{2,1,0:T(8,128)(2,1)S(1)}, bf16[2,24,1536]{2,1,0:T(8,128)(2,1)S(1)}, u32[]{:S(2)}, u32[]{:S(2)}) collective-permute-start(bf16[2,24,1536]{2,1,0:T(8,128)(2,1)S(1)} %activate.3.refs_0_), channel_id=1, source_target_pairs={{0,1},{1,0},{2,3},{3,2},{4,5},{5,4},{6,7},{7,6},{8,9},{9,8},{10,11... | collective-permute-start | bytes 442376 | tf_op jit(solution)/shard_map/ppermute | solution.py:58
  53.0 1.3 %collective-permute-start.10 = (bf16[4,3,1536]{2,1,0:T(4,128)(2,1)S(1)}, bf16[4,3,1536]{2,1,0:T(4,128)(2,1)S(1)}, u32[]{:S(2)}, u32[]{:S(2)}) collective-permute-start(bf16[4,3,1536]{2,1,0:T(4,128)(2,1)S(1)} %get-tuple-element.62), channel_id=1, source_target_pairs={{0,8},{4,12},{8,0},{12,4},{16,24},{20,28},{24,16},{28,20},{1,9},{5... | collective-permute-start | bytes 110600 | tf_op jit(solution)/shard_map/ppermute | solution.py:58
  54.4 7.7 %collective-permute-start.11 = (bf16[3,1536]{1,0:T(4,128)(2,1)S(1)}, bf16[3,1536]{1,0:T(4,128)(2,1)S(1)}, u32[]{:S(2)}, u32[]{:S(2)}) collective-permute-start(bf16[3,1536]{1,0:T(4,128)(2,1)S(1)} %get-tuple-element.64), channel_id=1, source_target_pairs={{0,4},{4,0},{8,12},{12,8},{16,20},{20,16},{24,28},{28,24},{1,5},{5... | collective-permute-start | bytes 27656 | tf_op jit(solution)/shard_map/ppermute | solution.py:58
  54.4 7.6 %collective-permute-start.12 = (bf16[3,1536]{1,0:T(4,128)(2,1)S(1)}, bf16[3,1536]{1,0:T(4,128)(2,1)S(1)}, u32[]{:S(2)}, u32[]{:S(2)}) collective-permute-start(bf16[3,1536]{1,0:T(4,128)(2,1)S(1)} %get-tuple-element.65), channel_id=1, source_target_pairs={{0,16},{4,20},{8,24},{12,28},{16,0},{20,4},{24,8},{28,12},{1,17},{... | collective-permute-start | bytes 27656 | tf_op jit(solution)/shard_map/ppermute | solution.py:58
  55.2 6.9 %collective-permute-start.13 = (bf16[3,1536]{1,0:T(4,128)(2,1)S(1)}, bf16[3,1536]{1,0:T(4,128)(2,1)S(1)}, u32[]{:S(2)}, u32[]{:S(2)}) collective-permute-start(bf16[3,1536]{1,0:T(4,128)(2,1)S(1)} %get-tuple-element.66), channel_id=1, source_target_pairs={{0,20},{4,16},{8,28},{12,24},{16,4},{20,0},{24,12},{28,8},{1,21},{... | collective-permute-start | bytes 27656 | tf_op jit(solution)/shard_map/ppermute | solution.py:58

commit v2 on v1

--- a/solution.py
+++ b/solution.py
@@ -201,28 +201,29 @@
     return pltpu.SemaphoreType.DMA((rows // PIECE, STRIPES))
 
 
-def load_kernel(other, quarter, up_ref, down_ref, _, up_kept, down_kept, up_sems, down_sems):
-    size = up_kept.shape[1]
-    base = first_unit(other, quarter, size)
-    copies = up_copies(base, size, up_ref, up_kept, up_sems)
-    copies += down_copies(base, size, down_ref, down_kept, down_sems)
+def load_kernel(up_ref, down_ref, _, *refs):
+    *up_kept, down_kept, first_sems, second_sems, down_sems = refs
+    size = down_kept.shape[0]
+    copies = up_copies(first_unit(1, 0, size), size, up_ref, up_kept[0], first_sems)
+    copies += down_copies(first_unit(1, 0, size), size, down_ref, down_kept, down_sems)
+    copies += up_copies(first_unit(1, 1, size), size, up_ref, up_kept[1], second_sems)
     for copy in copies:
         copy.start()
     for copy in copies:
         copy.wait()
 
 
-def load(w_up, w_down, other, quarter, after):
+def load(w_up, w_down, after):
     width, units = w_up.shape
     size = units // 4
     return pl.pallas_call(
-        functools.partial(load_kernel, other, quarter),
+        load_kernel,
         in_specs=anywhere(3),
-        out_specs=in_vmem(2),
-        out_shape=[pltpu.VMEM((width, size), BF16), pltpu.VMEM((size, width), BF16)],
-        scratch_shapes=[copy_sems(width), copy_sems(size)],
-        compiler_params=pltpu.CompilerParams(vmem_limit_bytes=SMALL),
-        cost_estimate=cost(0, 4 * width * size),
+        out_specs=in_vmem(3),
+        out_shape=[pltpu.VMEM((width, size), BF16)] * 2 + [pltpu.VMEM((size, width), BF16)],
+        scratch_shapes=[copy_sems(width), copy_sems(width), copy_sems(size)],
+        compiler_params=pltpu.CompilerParams(vmem_limit_bytes=SMALL),
+        cost_estimate=cost(0, 6 * width * size),
         name="load",
     )(keep_in(pltpu.HBM, w_up), keep_in(pltpu.HBM, w_down), after)
 
@@ -241,39 +242,30 @@
     out_ref[0] = pre_act.astype(out_ref.dtype)
 
 
-def forward_other_kernel(rows_ref, cot_ref, up_first, down_first, up_ref, down_ref, *refs):
-    first_out, second_out, up_kept, down_buf, *sems = refs
-    size = up_kept.shape[1]
-    base = first_unit(1, 1, size)
-    ups = up_copies(base, size, up_ref, up_kept, sems[0])
-    downs = down_copies(base, size, down_ref, down_buf, sems[1])
-    for pair in zip(ups, downs):
-        for copy in pair:
-            copy.start()
+def forward_other_kernel(rows_ref, cot_ref, up_first, up_second, down_first, down_ref, *refs):
+    first_out, second_out, down_buf, sems = refs
+    size = down_buf.shape[0]
+    downs = down_copies(first_unit(1, 1, size), size, down_ref, down_buf, sems)
+    for copy in downs:
+        copy.start()
     multiply(rows_ref, cot_ref, up_first, down_first, first_out)
-    multiply(rows_ref, cot_ref, up_kept, down_buf, second_out, ups, downs)
-
-
-def forward_other(rows, cot, up_first, down_first, w_up, w_down):
+    multiply(rows_ref, cot_ref, up_second, down_buf, second_out, (), downs)
+
+
+def forward_other(rows, cot, up_first, up_second, down_first, w_down):
     tokens, width = rows.shape
     size = up_first.shape[1]
+    kept = (keep_in(pltpu.VMEM, x) for x in (up_first, up_second, down_first))
     return pl.pallas_call(
         forward_other_kernel,
-        in_specs=in_vmem(4) + anywhere(2),
-        out_specs=in_vmem(3),
-        out_shape=[jax.ShapeDtypeStruct((2, tokens, size), BF16)] * 2 + [pltpu.VMEM((width, size), BF16)],
-        scratch_shapes=[pltpu.VMEM((size, width), BF16), copy_sems(width), copy_sems(size)],
+        in_specs=in_vmem(5) + anywhere(),
+        out_specs=in_vmem(2),
+        out_shape=[jax.ShapeDtypeStruct((2, tokens, size), BF16)] * 2,
+        scratch_shapes=[pltpu.VMEM((size, width), BF16), copy_sems(size)],
         compiler_params=pltpu.CompilerParams(vmem_limit_bytes=12 * MIB),
-        cost_estimate=cost(8 * tokens * width * size, 4 * width * size),
+        cost_estimate=cost(8 * tokens * width * size, 2 * width * size),
         name="forward_other",
-    )(
-        rows,
-        cot,
-        keep_in(pltpu.VMEM, up_first),
-        keep_in(pltpu.VMEM, down_first),
-        keep_in(pltpu.HBM, w_up),
-        keep_in(pltpu.HBM, w_down),
-    )
+    )(rows, cot, *kept, keep_in(pltpu.HBM, w_down))
 
 
 def forward_own_kernel(quarter, rows_ref, cot_ref, up_ref, down_ref, *refs):
@@ -457,10 +449,10 @@
     both = join(tokens, cotangent)
     both = pack([both, swap(both, group, owners, core)] if core else [both])
     kept, parts, sums, acts = {}, {}, {}, {}
-    kept[1, 0], down_first = load(w_up, w_down, 1, 0, after=both)
+    kept[1, 0], kept[1, 1], down_first = load(w_up, w_down, after=both)
     rows, cot, turned = unpack([both] + [swap(both, group, owners, at) for at in chips[1:]])
 
-    parts[1, 0], parts[1, 1], kept[1, 1] = forward_other(rows, cot, kept[1, 0], down_first, w_up, w_down)
+    parts[1, 0], parts[1, 1] = forward_other(rows, cot, kept[1, 0], kept[1, 1], down_first, w_down)
     theirs = [swap(parts[1, quarter], "gz", splits, 1) for quarter in (0, 1)]
     parts[0, 0], kept[0, 0] = forward_own(rows, cot, w_up, w_down, 0, after=(parts[1, 0],))
     sums[0], sent = pair_sums(parts[0, 0], theirs[0])

time: 63 us -> 61.7 us (0.979)
  waiting for transfers between devices: 7.92 us -> 6.38 us
  starting transfers between devices: 14 us -> 13.3 us
    ppermute x14, waiting for transfers between devices: 7.92 us -> 6.38 us  [swap(): return lax.ppermute(value, axes, [(i, i ^ at) for i in range(size)])]
    ppermute x14, starting transfers between devices: 14 us -> 13.3 us  [swap(): return lax.ppermute(value, axes, [(i, i ^ at) for i in range(size)])]
  transfers between devices with their start and end apart: 14 -> 14, of which waited for: 5 -> 6; matrix products, arithmetic and copies ran while one was open for 0% -> 0% of each run, Pallas kernels for 48% -> 51%
where the time goes in v2:
time: 61.7 us; the launch traced here: 61 us
  Pallas kernels  40.4 us (65%)
  starting transfers between devices  13.3 us (22%)
  waiting for transfers between devices  6.38 us (10%)
  between operations  0.83 us (1%)
    pallas_call x4, Pallas kernels, grads(): pl.pallas_call(functools.partial(grads_kernel, places, shared, bool(total...  16.7 us
    ppermute x14, starting transfers between devices, swap(): return lax.ppermute(value, axes, [(i, i ^ at) for i in range(size)])  13.3 us
    pallas_call x2, Pallas kernels, forward_own(): pl.pallas_call(functools.partial(forward_own_kernel, quarter), in_specs=i...  9.14 us
    ppermute x14, waiting for transfers between devices, swap(): return lax.ppermute(value, axes, [(i, i ^ at) for i in range(size)])  6.38 us
    pallas_call x1, Pallas kernels, forward_other(): pl.pallas_call(forward_other_kernel, in_specs=in_vmem(5) + anywhere(), ou...  5.93 us
    pallas_call x1, Pallas kernels, load(): pl.pallas_call(load_kernel, in_specs=anywhere(3), out_specs=in_vmem(3), o...  5.21 us
    pallas_call x1, Pallas kernels, grad_in_parts(): pl.pallas_call(grad_in_kernel, in_specs=in_vmem(3), out_specs=in_vmem(cor...  1.49 us
  transfers between devices with their start and end apart: 14, of which 6 were waited for; matrix products, arithmetic and copies ran while one was open for 0% of the time, Pallas kernels for 51%

profile of v2, /device:TPU:24, one launch (start us, length us, event | category | flops | bytes accessed | tf_op | source)
XLA Modules:
  0.0 61.0 jit_solution(7945650776186522823)
XLA Ops:
  0.6 0.7 %join.1.refs_0_ = bf16[2,3,1536]{2,1,0:T(4,128)(2,1)S(1)} custom-call(bf16[3,1536]{1,0:T(4,128)(2,1)} %tokens_ref.1, bf16[3,1536]{1,0:T(4,128)(2,1)} %cot_ref.1), custom_call_target="tpu_custom_call" | custom-call | tf_op jit(solution)/shard_map/join/pallas_call | solution.py:100
  1.4 0.1 collective-permute-start
  1.5 1.2 %collective-permute-done.refs_1_ = bf16[2,3,1536]{2,1,0:T(4,128)(2,1)S(1)} collective-permute-done((bf16[2,3,1536]{2,1,0:T(4,128)(2,1)S(1)}, bf16[2,3,1536]{2,1,0:T(4,128)(2,1)S(1)}, u32[]{:S(2)}, u32[]{:S(2)}) %collective-permute-start) | collective-permute-done | bytes 18464 | tf_op jit(solution)/shard_map/ppermute | solution.py:58
  2.7 1.6 %collective-permute-start.1 = (bf16[2,2,3,1536]{3,2,1,0:T(4,128)(2,1)S(1)}, bf16[2,2,3,1536]{3,2,1,0:T(4,128)(2,1)S(1)}, u32[]{:S(2)}, u32[]{:S(2)}) collective-permute-start(bf16[2,2,3,1536]{3,2,1,0:T(4,128)(2,1)S(1)} %pack.1.refs_0_._), channel_id=1, source_target_pairs={{0,4},{4,0},{8,12},{12,8},{16,20},{20,16},{24,28},{28,24},{1,5},{5... | collective-permute-start | bytes 110600 | tf_op jit(solution)/shard_map/ppermute | solution.py:58
  4.2 1.5 %collective-permute-start.2 = (bf16[2,2,3,1536]{3,2,1,0:T(4,128)(2,1)S(1)}, bf16[2,2,3,1536]{3,2,1,0:T(4,128)(2,1)S(1)}, u32[]{:S(2)}, u32[]{:S(2)}) collective-permute-start(bf16[2,2,3,1536]{3,2,1,0:T(4,128)(2,1)S(1)} %pack.1.refs_0_._), channel_id=1, source_target_pairs={{0,16},{4,20},{8,24},{12,28},{16,0},{20,4},{24,8},{28,12},{1,17},{... | collective-permute-start | bytes 110600 | tf_op jit(solution)/shard_map/ppermute | solution.py:58
  5.7 0.5 collective-permute-start.3
  6.2 5.2 %load.1 = (bf16[1536,1536]{1,0:T(8,128)(2,1)S(1)}, bf16[1536,1536]{1,0:T(8,128)(2,1)S(1)}, bf16[1536,1536]{1,0:T(8,128)(2,1)S(1)}) custom-call(bf16[1536,6144]{1,0:T(8,128)(2,1)} %up_ref.5, bf16[6144,1536]{1,0:T(8,128)(2,1)} %down_ref.7, bf16[2,2,3,1536]{3,2,1,0:T(4,128)(2,1)S(1)} %pack.1.refs_0_._), custom_call_target="tpu_custom_call" | custom-call | bytes 14155776 | tf_op jit(solution)/shard_map/load/pallas_call | solution.py:219
  11.5 0.2 unpack.1
  11.7 5.9 %forward_other.1 = (bf16[2,24,1536]{2,1,0:T(8,128)(2,1)S(1)}, bf16[2,24,1536]{2,1,0:T(8,128)(2,1)S(1)}) custom-call(bf16[24,1536]{1,0:T(8,128)(2,1)S(1)} %get-tuple-element.39.rows_ref, bf16[24,1536]{1,0:T(8,128)(2,1)S(1)} %get-tuple-element.38.cot_ref, bf16[1536,1536]{1,0:T(8,128)(2,1)S(1)} %get-tuple-element.40.up_first.refs_1_, ...), custom_call_target="tpu_custom_call" | custom-call | flops 452984832 | bytes 4718592 | tf_op jit(solution)/shard_map/forward_other/pallas_call | solution.py:259
  17.6 0.5 collective-permute-start.4
  18.2 1.6 %collective-permute-start.6 = (bf16[2,24,1536]{2,1,0:T(8,128)(2,1)S(1)}, bf16[2,24,1536]{2,1,0:T(8,128)(2,1)S(1)}, u32[]{:S(2)}, u32[]{:S(2)}) collective-permute-start(bf16[2,24,1536]{2,1,0:T(8,128)(2,1)S(1)} %get-tuple-element.47), channel_id=1, source_target_pairs={{0,1},{1,0},{2,3},{3,2},{4,5},{5,4},{6,7},{7,6},{8,9},{9,8},{10,11... | collective-permute-start | bytes 442376 | tf_op jit(solution)/shard_map/ppermute | solution.py:58
  19.7 4.6 %forward_own.2 = (f32[2,24,1536]{2,1,0:T(8,128)S(1)}, bf16[1536,1536]{1,0:T(8,128)(2,1)S(1)}) custom-call(bf16[24,1536]{1,0:T(8,128)(2,1)S(1)} %get-tuple-element.39.rows_ref, bf16[24,1536]{1,0:T(8,128)(2,1)S(1)} %get-tuple-element.38.cot_ref, bf16[1536,6144]{1,0:T(8,128)(2,1)} %up_ref.5, bf16[6144,1536]{1,0:T(8,128)(2,1)} %down_ref.7, ...), custom_call_target="tpu_custom_call" | custom-call | flops 226492416 | bytes 9437184 | tf_op jit(solution)/shard_map/forward_own/pallas_call | solution.py:286
  24.4 0.4 collective-permute-start.5
  24.8 1.1 %collective-permute-done.6.refs_1_.arrived_ref = bf16[2,24,1536]{2,1,0:T(8,128)(2,1)S(1)} collective-permute-done((bf16[2,24,1536]{2,1,0:T(8,128)(2,1)S(1)}, bf16[2,24,1536]{2,1,0:T(8,128)(2,1)S(1)}, u32[]{:S(2)}, u32[]{:S(2)}) %collective-permute-start.6) | collective-permute-done | bytes 147488 | tf_op jit(solution)/shard_map/ppermute | solution.py:58
  25.9 4.6 %forward_own.3 = (f32[2,24,1536]{2,1,0:T(8,128)S(1)}, bf16[1536,1536]{1,0:T(8,128)(2,1)S(1)}) custom-call(bf16[24,1536]{1,0:T(8,128)(2,1)S(1)} %get-tuple-element.39.rows_ref, bf16[24,1536]{1,0:T(8,128)(2,1)S(1)} %get-tuple-element.38.cot_ref, bf16[1536,6144]{1,0:T(8,128)(2,1)} %up_ref.5, bf16[6144,1536]{1,0:T(8,128)(2,1)} %down_ref.7, ...), custom_call_target="tpu_custom_call" | custom-call | flops 226492416 | bytes 9437184 | tf_op jit(solution)/shard_map/forward_own/pallas_call | solution.py:286
  30.6 1.5 %collective-permute-start.8 = (bf16[2,24,1536]{2,1,0:T(8,128)(2,1)S(1)}, bf16[2,24,1536]{2,1,0:T(8,128)(2,1)S(1)}, u32[]{:S(2)}, u32[]{:S(2)}) collective-permute-start(bf16[2,24,1536]{2,1,0:T(8,128)(2,1)S(1)} %get-tuple-element.49.refs_0_), channel_id=1, source_target_pairs={{0,2},{1,3},{2,0},{3,1},{4,6},{5,7},{6,4},{7,5},{8,10},{9,11},{10,... | collective-permute-start | bytes 442376 | tf_op jit(solution)/shard_map/ppermute | solution.py:58
  32.1 2.7 %collective-permute-done.5.arrived_ref = bf16[2,24,1536]{2,1,0:T(8,128)(2,1)S(1)} collective-permute-done((bf16[2,24,1536]{2,1,0:T(8,128)(2,1)S(1)}, bf16[2,24,1536]{2,1,0:T(8,128)(2,1)S(1)}, u32[]{:S(2)}, u32[]{:S(2)}) %collective-permute-start.5) | collective-permute-done | bytes 147488 | tf_op jit(solution)/shard_map/ppermute | solution.py:58
  34.8 0.1 activate.2.refs_0_
  34.9 4.1 %grads.4 = (bf16[1536,6144]{1,0:T(8,128)(2,1)}, bf16[6144,1536]{1,0:T(8,128)(2,1)}, f32[24,1536]{1,0:T(8,128)S(1)}, bf16[2,24,1536]{2,1,0:T(8,128)(2,1)S(1)}) custom-call(bf16[1536,24]{1,0:T(8,128)(2,1)S(1)} %get-tuple-element.37.turned_ref, bf16[24,1536]{1,0:T(8,128)(2,1)S(1)} %get-tuple-element.38.cot_ref, bf16[2,24,1536]{2,1,0:T(8,128)(2,1)S(1)} %activate.2.refs_0_, ...), custom_call_target="tpu_custom_call" | custom-call | flops 339738624 | bytes 9437184 | tf_op jit(solution)/shard_map/grads/pallas_call | solution.py:365
  39.1 0.1 collective-permute-start.7
  39.2 0.1 collective-permute-done.8.arrived_ref
  39.2 0.1 activate.3.refs_0_
  39.4 2.0 %collective-permute-start.9 = (bf16[2,24,1536]{2,1,0:T(8,128)(2,1)S(1)}, bf16[2,24,1536]{2,1,0:T(8,128)(2,1)S(1)}, u32[]{:S(2)}, u32[]{:S(2)}) collective-permute-start(bf16[2,24,1536]{2,1,0:T(8,128)(2,1)S(1)} %activate.3.refs_0_), channel_id=1, source_target_pairs={{0,1},{1,0},{2,3},{3,2},{4,5},{5,4},{6,7},{7,6},{8,9},{9,8},{10,11... | collective-permute-start | bytes 442376 | tf_op jit(solution)/shard_map/ppermute | solution.py:58
  41.4 4.3 %grads.5 = (bf16[1536,6144]{1,0:T(8,128)(2,1)}, bf16[6144,1536]{1,0:T(8,128)(2,1)}, f32[24,1536]{1,0:T(8,128)S(1)}) custom-call(bf16[1536,24]{1,0:T(8,128)(2,1)S(1)} %get-tuple-element.37.turned_ref, bf16[24,1536]{1,0:T(8,128)(2,1)S(1)} %get-tuple-element.38.cot_ref, ...), custom_call_target="tpu_custom_call", output_to_operand_aliasing={{0}: (5, {}), {1}: (6, {})} | custom-call | flops 339738624 | bytes 9437184 | tf_op jit(solution)/shard_map/grads/pallas_call | solution.py:365
  45.7 4.1 %grads.6 = (bf16[1536,6144]{1,0:T(8,128)(2,1)}, bf16[6144,1536]{1,0:T(8,128)(2,1)}, f32[24,1536]{1,0:T(8,128)S(1)}) custom-call(bf16[1536,24]{1,0:T(8,128)(2,1)S(1)} %get-tuple-element.37.turned_ref, bf16[24,1536]{1,0:T(8,128)(2,1)S(1)} %get-tuple-element.38.cot_ref, ...), custom_call_target="tpu_custom_call", output_to_operand_aliasing={{0}: (5, {}), {1}: (6, {})} | custom-call | flops 339738624 | bytes 9437184 | tf_op jit(solution)/shard_map/grads/pallas_call | solution.py:365
  49.8 1.5 %grad_in.1 = (bf16[4,3,1536]{2,1,0:T(4,128)(2,1)S(1)}, bf16[4,3,1536]{2,1,0:T(4,128)(2,1)S(1)}) custom-call(f32[24,1536]{1,0:T(8,128)S(1)} %get-tuple-element.60.total_ref, bf16[2,24,1536]{2,1,0:T(8,128)(2,1)S(1)} %collective-permute-done.9.acts_ref.refs_0_, bf16[1536,1536]{1,0:T(8,128)(2,1)S(1)} %get-tuple-element.41.up_second.up_ref), custom_call_target="tpu_custom_call" | custom-call | flops 113246208 | bytes 4718592 | tf_op jit(solution)/shard_map/grad_in/pallas_call | solution.py:397
  51.4 1.2 %collective-permute-done.10.refs_1_ = bf16[4,3,1536]{2,1,0:T(4,128)(2,1)S(1)} collective-permute-done((bf16[4,3,1536]{2,1,0:T(4,128)(2,1)S(1)}, bf16[4,3,1536]{2,1,0:T(4,128)(2,1)S(1)}, u32[]{:S(2)}, u32[]{:S(2)}) %collective-permute-start.10) | collective-permute-done | bytes 36896 | tf_op jit(solution)/shard_map/ppermute | solution.py:58
  52.7 1.6 %collective-permute-start.11 = (bf16[3,1536]{1,0:T(4,128)(2,1)S(1)}, bf16[3,1536]{1,0:T(4,128)(2,1)S(1)}, u32[]{:S(2)}, u32[]{:S(2)}) collective-permute-start(bf16[3,1536]{1,0:T(4,128)(2,1)S(1)} %get-tuple-element.64), channel_id=1, source_target_pairs={{0,4},{4,0},{8,12},{12,8},{16,20},{20,16},{24,28},{28,24},{1,5},{5... | collective-permute-start | bytes 27656 | tf_op jit(solution)/shard_map/ppermute | solution.py:58
  54.2 1.5 %collective-permute-start.12 = (bf16[3,1536]{1,0:T(4,128)(2,1)S(1)}, bf16[3,1536]{1,0:T(4,128)(2,1)S(1)}, u32[]{:S(2)}, u32[]{:S(2)}) collective-permute-start(bf16[3,1536]{1,0:T(4,128)(2,1)S(1)} %get-tuple-element.65), channel_id=1, source_target_pairs={{0,16},{4,20},{8,24},{12,28},{16,0},{20,4},{24,8},{28,12},{1,17},{... | collective-permute-start | bytes 27656 | tf_op jit(solution)/shard_map/ppermute | solution.py:58
  55.7 0.5 collective-permute-start.13
  56.2 4.1 %grads.7 = (bf16[1536,6144]{1,0:T(8,128)(2,1)}, bf16[6144,1536]{1,0:T(8,128)(2,1)}) custom-call(bf16[1536,24]{1,0:T(8,128)(2,1)S(1)} %get-tuple-element.37.turned_ref, bf16[24,1536]{1,0:T(8,128)(2,1)S(1)} %get-tuple-element.38.cot_ref, ...), custom_call_target="tpu_custom_call", output_to_operand_aliasing={{0}: (3, {}), {1}: (4, {})} | custom-call | flops 339738624 | bytes 9437184 | tf_op jit(solution)/shard_map/grads/pallas_call | solution.py:365
  60.4 0.6 %add_up.1 = f32[3,1536]{1,0:T(4,128)} custom-call(f32[3,1536]{1,0:T(4,128)S(1)} %get-tuple-element.63.refs_0_.refs_3_, bf16[3,1536]{1,0:T(4,128)(2,1)S(1)} %collective-permute-done.11.refs_1_, bf16[3,1536]{1,0:T(4,128)(2,1)S(1)} %collective-permute-done.12.refs_2_, bf16[3,1536]{1,0:T(4,128)(2,1)S(1)} %collective-permute-done.13.refs_3_), custom_call_target="tpu_custom_call" | custom-call | tf_op jit(solution)/shard_map/add_up/pallas_call | solution.py:158
  (14 shorter events, 0.3 us)
Async XLA Ops:
  1.4 1.3 %collective-permute-start = (bf16[2,3,1536]{2,1,0:T(4,128)(2,1)S(1)}, bf16[2,3,1536]{2,1,0:T(4,128)(2,1)S(1)}, u32[]{:S(2)}, u32[]{:S(2)}) collective-permute-start(bf16[2,3,1536]{2,1,0:T(4,128)(2,1)S(1)} %join.1.refs_0_), channel_id=1, source_target_pairs={{0,8},{4,12},{8,0},{12,4},{16,24},{20,28},{24,16},{28,20},{1,9},{5... | collective-permute-start | bytes 55304 | tf_op jit(solution)/shard_map/ppermute | solution.py:58
  2.7 8.8 %collective-permute-start.1 = (bf16[2,2,3,1536]{3,2,1,0:T(4,128)(2,1)S(1)}, bf16[2,2,3,1536]{3,2,1,0:T(4,128)(2,1)S(1)}, u32[]{:S(2)}, u32[]{:S(2)}) collective-permute-start(bf16[2,2,3,1536]{3,2,1,0:T(4,128)(2,1)S(1)} %pack.1.refs_0_._), channel_id=1, source_target_pairs={{0,4},{4,0},{8,12},{12,8},{16,20},{20,16},{24,28},{28,24},{1,5},{5... | collective-permute-start | bytes 110600 | tf_op jit(solution)/shard_map/ppermute | solution.py:58
  4.2 7.2 %collective-permute-start.2 = (bf16[2,2,3,1536]{3,2,1,0:T(4,128)(2,1)S(1)}, bf16[2,2,3,1536]{3,2,1,0:T(4,128)(2,1)S(1)}, u32[]{:S(2)}, u32[]{:S(2)}) collective-permute-start(bf16[2,2,3,1536]{3,2,1,0:T(4,128)(2,1)S(1)} %pack.1.refs_0_._), channel_id=1, source_target_pairs={{0,16},{4,20},{8,24},{12,28},{16,0},{20,4},{24,8},{28,12},{1,17},{... | collective-permute-start | bytes 110600 | tf_op jit(solution)/shard_map/ppermute | solution.py:58
  5.7 5.7 %collective-permute-start.3 = (bf16[2,2,3,1536]{3,2,1,0:T(4,128)(2,1)S(1)}, bf16[2,2,3,1536]{3,2,1,0:T(4,128)(2,1)S(1)}, u32[]{:S(2)}, u32[]{:S(2)}) collective-permute-start(bf16[2,2,3,1536]{3,2,1,0:T(4,128)(2,1)S(1)} %pack.1.refs_0_._), channel_id=1, source_target_pairs={{0,20},{4,16},{8,28},{12,24},{16,4},{20,0},{24,12},{28,8},{1,21},{... | collective-permute-start | bytes 110600 | tf_op jit(solution)/shard_map/ppermute | solution.py:58
  17.6 6.7 %collective-permute-start.4 = (bf16[2,24,1536]{2,1,0:T(8,128)(2,1)S(1)}, bf16[2,24,1536]{2,1,0:T(8,128)(2,1)S(1)}, u32[]{:S(2)}, u32[]{:S(2)}) collective-permute-start(bf16[2,24,1536]{2,1,0:T(8,128)(2,1)S(1)} %get-tuple-element.43.refs_0_), channel_id=1, source_target_pairs={{0,1},{1,0},{2,3},{3,2},{4,5},{5,4},{6,7},{7,6},{8,9},{9,8},{10,11... | collective-permute-start | bytes 442376 | tf_op jit(solution)/shard_map/ppermute | solution.py:58
  18.2 7.8 %collective-permute-start.6 = (bf16[2,24,1536]{2,1,0:T(8,128)(2,1)S(1)}, bf16[2,24,1536]{2,1,0:T(8,128)(2,1)S(1)}, u32[]{:S(2)}, u32[]{:S(2)}) collective-permute-start(bf16[2,24,1536]{2,1,0:T(8,128)(2,1)S(1)} %get-tuple-element.47), channel_id=1, source_target_pairs={{0,1},{1,0},{2,3},{3,2},{4,5},{5,4},{6,7},{7,6},{8,9},{9,8},{10,11... | collective-permute-start | bytes 442376 | tf_op jit(solution)/shard_map/ppermute | solution.py:58
  24.4 10.4 %collective-permute-start.5 = (bf16[2,24,1536]{2,1,0:T(8,128)(2,1)S(1)}, bf16[2,24,1536]{2,1,0:T(8,128)(2,1)S(1)}, u32[]{:S(2)}, u32[]{:S(2)}) collective-permute-start(bf16[2,24,1536]{2,1,0:T(8,128)(2,1)S(1)} %get-tuple-element.46.refs_0_), channel_id=1, source_target_pairs={{0,2},{1,3},{2,0},{3,1},{4,6},{5,7},{6,4},{7,5},{8,10},{9,11},{10,... | collective-permute-start | bytes 442376 | tf_op jit(solution)/shard_map/ppermute | solution.py:58
  30.6 8.7 %collective-permute-start.8 = (bf16[2,24,1536]{2,1,0:T(8,128)(2,1)S(1)}, bf16[2,24,1536]{2,1,0:T(8,128)(2,1)S(1)}, u32[]{:S(2)}, u32[]{:S(2)}) collective-permute-start(bf16[2,24,1536]{2,1,0:T(8,128)(2,1)S(1)} %get-tuple-element.49.refs_0_), channel_id=1, source_target_pairs={{0,2},{1,3},{2,0},{3,1},{4,6},{5,7},{6,4},{7,5},{8,10},{9,11},{10,... | collective-permute-start | bytes 442376 | tf_op jit(solution)/shard_map/ppermute | solution.py:58
  39.1 6.6 %collective-permute-start.7 = (bf16[2,24,1536]{2,1,0:T(8,128)(2,1)S(1)}, bf16[2,24,1536]{2,1,0:T(8,128)(2,1)S(1)}, u32[]{:S(2)}, u32[]{:S(2)}) collective-permute-start(bf16[2,24,1536]{2,1,0:T(8,128)(2,1)S(1)} %get-tuple-element.51), channel_id=1, source_target_pairs={{0,1},{1,0},{2,3},{3,2},{4,5},{5,4},{6,7},{7,6},{8,9},{9,8},{10,11... | collective-permute-start | bytes 442376 | tf_op jit(solution)/shard_map/ppermute | solution.py:58
  39.4 10.5 %collective-permute-start.9 = (bf16[2,24,1536]{2,1,0:T(8,128)(2,1)S(1)}, bf16[2,24,1536]{2,1,0:T(8,128)(2,1)S(1)}, u32[]{:S(2)}, u32[]{:S(2)}) collective-permute-start(bf16[2,24,1536]{2,1,0:T(8,128)(2,1)S(1)} %activate.3.refs_0_), channel_id=1, source_target_pairs={{0,1},{1,0},{2,3},{3,2},{4,5},{5,4},{6,7},{7,6},{8,9},{9,8},{10,11... | collective-permute-start | bytes 442376 | tf_op jit(solution)/shard_map/ppermute | solution.py:58
  51.3 1.3 %collective-permute-start.10 = (bf16[4,3,1536]{2,1,0:T(4,128)(2,1)S(1)}, bf16[4,3,1536]{2,1,0:T(4,128)(2,1)S(1)}, u32[]{:S(2)}, u32[]{:S(2)}) collective-permute-start(bf16[4,3,1536]{2,1,0:T(4,128)(2,1)S(1)} %get-tuple-element.62), channel_id=1, source_target_pairs={{0,8},{4,12},{8,0},{12,4},{16,24},{20,28},{24,16},{28,20},{1,9},{5... | collective-permute-start | bytes 110600 | tf_op jit(solution)/shard_map/ppermute | solution.py:58
  52.7 7.7 %collective-permute-start.11 = (bf16[3,1536]{1,0:T(4,128)(2,1)S(1)}, bf16[3,1536]{1,0:T(4,128)(2,1)S(1)}, u32[]{:S(2)}, u32[]{:S(2)}) collective-permute-start(bf16[3,1536]{1,0:T(4,128)(2,1)S(1)} %get-tuple-element.64), channel_id=1, source_target_pairs={{0,4},{4,0},{8,12},{12,8},{16,20},{20,16},{24,28},{28,24},{1,5},{5... | collective-permute-start | bytes 27656 | tf_op jit(solution)/shard_map/ppermute | solution.py:58
  54.2 6.1 %collective-permute-start.12 = (bf16[3,1536]{1,0:T(4,128)(2,1)S(1)}, bf16[3,1536]{1,0:T(4,128)(2,1)S(1)}, u32[]{:S(2)}, u32[]{:S(2)}) collective-permute-start(bf16[3,1536]{1,0:T(4,128)(2,1)S(1)} %get-tuple-element.65), channel_id=1, source_target_pairs={{0,16},{4,20},{8,24},{12,28},{16,0},{20,4},{24,8},{28,12},{1,17},{... | collective-permute-start | bytes 27656 | tf_op jit(solution)/shard_map/ppermute | solution.py:58
  55.7 4.7 %collective-permute-start.13 = (bf16[3,1536]{1,0:T(4,128)(2,1)S(1)}, bf16[3,1536]{1,0:T(4,128)(2,1)S(1)}, u32[]{:S(2)}, u32[]{:S(2)}) collective-permute-start(bf16[3,1536]{1,0:T(4,128)(2,1)S(1)} %get-tuple-element.66), channel_id=1, source_target_pairs={{0,20},{4,16},{8,28},{12,24},{16,4},{20,0},{24,12},{28,8},{1,21},{... | collective-permute-start | bytes 27656 | tf_op jit(solution)/shard_map/ppermute | solution.py:58
